TPU v7x, 32 devices: a whole 2x2x4 slice. The times are simulated.
32 devices in a mesh: seq: 2 (over y), pos: 16 (over z, x, core).
Axes of the slice: x: 2, y: 2, z: 4, core: 2. Of those that a mesh axis runs over, the one named last changes fastest.
Arguments:
- states: int32 [256, 256], P('seq', 'pos'), may hold values from 0 to 20
- multiplicity: int32 [256], P('seq'), may hold values from 1 to 8
- fields: float32 [256, 21], P('pos'), may hold values from -3 to 360
- diag_couplings: float32 [16, 336, 336], P('pos'), may hold values from -12 to 12
- slot_couplings: float32 [16, 4, 336, 336], P('pos'), may hold values from -12 to 12
- slot_blocks: int32 [16, 4], replicated, may hold values from -1 to 15, as said below
- partner_blocks: int32 [16, 4], replicated, may hold values from -1 to 15, as said below
Outputs:
- new_fields: float32 [256, 21], P('pos')
- new_diag: float32 [16, 336, 336], P('pos')
- new_slots: float32 [16, 4, 336, 336], P('pos')
Inputs may be any that keep to these rules, and one draw needn't show every extreme that they name: slot_blocks[c, t] is the block whose conditionals use the couplings in slot t of block c, or -1 for an empty slot. Slot 0 holds c - 1 and slot 1 holds c + 1 where such a block exists; the other slots hold blocks at least two away from c; no block stands twice in one row or in one column. partner_blocks[b] lists candidate partner blocks of block b, or -1: entry 0 is b - 1 and entry 1 is b + 1 where they exist; entry t >= 2 is -1 or the block c with slot_blocks[c, t] = b.
All inputs are finite; a program needn't handle non-finite values.
Results may differ from a plain program's by a relative error of at most 0.0025.
Values may be sent and summed in bfloat16 or wider, within the bound.
A program may use at most 64 MiB of HBM per device.

v0:
```python
import jax
import jax.numpy as jnp
from jax import lax
from jax.sharding import PartitionSpec as P

STEP_SIZE = 0.2
THRESHOLD = 0.3
HIGHEST_MODE = lax.Precision.HIGHEST


def shrink_whole(values, block_len, states_count):
    leading = values.shape[:-2]
    grouped = values.reshape(leading + (block_len, states_count, block_len, states_count))
    square_sums = jnp.sum(grouped * grouped, axis=(-3, -1), keepdims=True)
    factor = jnp.maximum(0.0, 1.0 - THRESHOLD / jnp.sqrt(square_sums + 1e-06))
    return (grouped * factor).reshape(values.shape)


def per_device(
    states, multiplicity, fields, diag_couplings, slot_couplings, slot_blocks, partner_blocks
):
    seq_rows, block_len = states.shape
    states_count = fields.shape[1]
    row_width = block_len * states_count
    blocks = lax.axis_size("pos")
    my_block = lax.axis_index("pos")
    onehot_rows = jax.nn.one_hot(states, states_count, dtype=jnp.bfloat16).reshape(
        seq_rows, row_width
    )
    onehot_wide = onehot_rows.astype(jnp.float32)
    weight = 1.0 / multiplicity.astype(jnp.float32)
    position = jnp.arange(row_width) // states_count
    off_self = (position[:, None] != position[None, :]).astype(jnp.float32)
    block_ids = jnp.arange(blocks, dtype=jnp.int32)
    holder_match = slot_blocks[:, :, None, None] == block_ids[None, None, :, None]
    lister_match = partner_blocks[None, None, :, :] == block_ids[:, None, None, None]
    listed = jnp.any(holder_match & lister_match, axis=(2, 3))
    alive_table = (slot_blocks >= 0) & listed
    routing = (slot_blocks.T[:, :, None] == block_ids[None, None, :]) & alive_table.T[:, :, None]
    route_pick = routing.astype(jnp.bfloat16)
    slot_pick = lax.dynamic_index_in_dim(route_pick, my_block, axis=1, keepdims=False)
    alive_slots = lax.dynamic_index_in_dim(alive_table, my_block, axis=0, keepdims=False).astype(
        jnp.float32
    )
    slot_terms = jnp.einsum(
        "nk,tik->tni", onehot_wide, slot_couplings[0], precision=HIGHEST_MODE
    ).astype(jnp.bfloat16)
    outgoing = jnp.einsum("td,tnk->dnk", slot_pick, slot_terms, preferred_element_type=jnp.bfloat16)
    arrived = lax.all_to_all(outgoing, "pos", split_axis=0, concat_axis=0, tiled=True)
    source_ones = jnp.ones((arrived.shape[0],), jnp.bfloat16)
    incoming = jnp.einsum("d,dnk->nk", source_ones, arrived, preferred_element_type=jnp.float32)
    own_terms = jnp.einsum(
        "nk,ik->ni", onehot_wide, diag_couplings[0] * off_self, precision=HIGHEST_MODE
    )
    logits = fields.reshape(1, row_width) + own_terms + incoming
    probabilities = jax.nn.softmax(
        logits.reshape(seq_rows, block_len, states_count), axis=-1
    ).reshape(seq_rows, row_width)
    residual = (weight[:, None] * (probabilities - onehot_wide)).astype(jnp.bfloat16)
    row_ones = jnp.ones((1, seq_rows), jnp.bfloat16)
    grad_fields = jnp.dot(row_ones, residual, preferred_element_type=jnp.float32).reshape(
        block_len, states_count
    )
    grad_diag = jnp.einsum("ni,nk->ik", residual, onehot_rows, preferred_element_type=jnp.float32)
    holders = jnp.max(
        lax.dynamic_index_in_dim(route_pick, my_block, axis=2, keepdims=False), axis=0
    )
    sending = holders[:, None, None] * residual[None, :, :]
    arrived_resid = lax.all_to_all(sending, "pos", split_axis=0, concat_axis=0, tiled=True)
    picked = jnp.einsum(
        "td,dnk->tnk", slot_pick, arrived_resid, preferred_element_type=jnp.bfloat16
    )
    grad_slots = jnp.einsum("tni,nk->tik", picked, onehot_rows, preferred_element_type=jnp.float32)
    grad_diag, grad_slots, grad_fields = lax.psum((grad_diag, grad_slots, grad_fields), "seq")
    new_diag = off_self * shrink_whole(
        diag_couplings[0] - STEP_SIZE * grad_diag, block_len, states_count
    )
    new_slots = alive_slots[:, None, None] * shrink_whole(
        slot_couplings[0] - STEP_SIZE * grad_slots, block_len, states_count
    )
    new_fields = fields - STEP_SIZE * grad_fields
    return (new_fields, new_diag[None], new_slots[None])


def solution(mesh):
    placed = (
        P("seq", "pos"),
        P("seq"),
        P("pos", None),
        P("pos", None, None),
        P("pos", None, None, None),
        P(),
        P(),
    )
    return jax.shard_map(
        per_device,
        mesh=mesh,
        in_specs=placed,
        out_specs=(P("pos", None), P("pos", None, None), P("pos", None, None, None)),
        check_vma=False,
    )
```

profile of v0, /device:TPU:0, one launch (start us, length us, event | category | flops | bytes accessed | tf_op | source)
XLA Modules:
  0.0 227.3 jit_solution(8267558726213471596)
XLA Ops:
  7.2 0.7 iota_compare_fusion.1
  7.9 0.8 iota_compare_fusion.2
  8.6 0.8 copy.34
  9.5 0.7 compare_and_fusion
  10.3 0.7 iota_compare_fusion
  11.2 2.6 %fusion.10 = bf16[4,128,336]{1,2,0:T(8,128)(2,1)S(1)} fusion(pred[128,336,1]{0,1,2:T(8,128)(4,1)S(1)} %reshape.213, f32[1,4,336,336]{3,2,1,0:T(8,128)} %param.11), kind=kOutput, calls=%fused_computation.10 | convolution fusion | flops 693805056 | bytes 2193408 | tf_op jit(solution)/shard_map/nk,tik->tni/dot_general | solution.py:45
  13.8 0.6 fusion.20
  14.4 1.4 copy.37
  15.9 7.5 %all-to-all-start = ((bf16[16,128,336]{1,2,0:T(8,128)(2,1)}), bf16[16,128,336]{1,2,0:T(8,128)(2,1)S(1)}, u32[]{:S(2)}, u32[]{:S(2)}) async-start(bf16[16,128,336]{1,2,0:T(8,128)(2,1)} %copy.37), calls=%async_computation | async-start | bytes 2752512 | tf_op jit(solution)/shard_map/all_to_all | solution.py:49
  24.0 27.9 %all-to-all-done = bf16[16,128,336]{1,2,0:T(8,128)(2,1)S(1)} async-done(((bf16[16,128,336]{1,2,0:T(8,128)(2,1)}), bf16[16,128,336]{1,2,0:T(8,128)(2,1)S(1)}, u32[]{:S(2)}, u32[]{:S(2)}) %all-to-all-start) | async-done | bytes 1376288 | tf_op jit(solution)/shard_map/all_to_all | solution.py:49
  52.3 0.4 fusion.13
  52.8 0.5 fusion
  53.5 1.2 broadcast_multiply_fusion
  54.8 8.3 %all-to-all-start.1 = ((bf16[16,128,336]{1,2,0:T(8,128)(2,1)}), bf16[16,128,336]{1,2,0:T(8,128)(2,1)S(1)}, u32[]{:S(2)}, u32[]{:S(2)}) async-start(bf16[16,128,336]{1,2,0:T(8,128)(2,1)} %broadcast_multiply_fusion), calls=%async_computation.1 | async-start | bytes 2752512 | tf_op jit(solution)/shard_map/all_to_all | solution.py:69
  63.1 1.0 fusion.43
  64.1 27.5 %all-to-all-done.1 = bf16[16,128,336]{1,2,0:T(8,128)(2,1)S(1)} async-done(((bf16[16,128,336]{1,2,0:T(8,128)(2,1)}), bf16[16,128,336]{1,2,0:T(8,128)(2,1)S(1)}, u32[]{:S(2)}, u32[]{:S(2)}) %all-to-all-start.1) | async-done | bytes 1376288 | tf_op jit(solution)/shard_map/all_to_all | solution.py:69
  92.0 1.7 fusion.18
  94.2 5.1 %psum.21 = f32[16,21]{1,0:T(8,128)S(1)} all-reduce(f32[16,21]{1,0:T(8,128)S(1)} %bitcast.67), channel_id=1, replica_groups=mesh['seq'=2,'pos'=16] {'seq'}, use_global_device_ids=true, to_apply=%region_3.4 | all-reduce | flops 336 | bytes 2688 | tf_op jit(solution)/shard_map/psum | solution.py:74
  99.4 0.6 multiply_subtract_fusion
  100.0 71.2 %all-reduce.3.cloned.1.call-done = (f32[336,336]{1,0:T(8,128)}, f32[4,336,336]{2,1,0:T(8,128)}) async-done(((f32[336,336]{1,0:T(8,128)}, f32[4,336,336]{2,1,0:T(8,128)}), (f32[336,336]{1,0:T(8,128)}, f32[4,336,336]{2,1,0:T(8,128)})) %all-reduce.3.cloned.1.call-update) | async-done | bytes 2257936 | tf_op jit(solution)/shard_map/psum | solution.py:74
  171.2 1.1 fusion.25
  172.3 3.1 %fusion.14 = f32[4,336,336]{2,1,0:T(8,128)} fusion(f32[4,336,336]{2,1,0:T(8,128)} %get-tuple-element.4, f32[1,4,336,336]{3,2,1,0:T(8,128)S(1)} %copy-done), kind=kLoop, calls=%fused_computation.13 | loop fusion | flops 1354752 | bytes 5419008 | tf_op jit(solution)/shard_map/mul | solution.py:14
  175.4 3.3 %mul.98 = f32[16,21,16,21]{3,2,1,0:T(8,128)} reshape(f32[336,336]{1,0:T(8,128)S(1)} %fusion.25) | data formatting | bytes 903168 | tf_op jit(solution)/shard_map/mul | solution.py:14
  178.6 2.0 reduce_sum.28
  180.7 1.8 mul.99
  182.5 3.5 %mul.100 = f32[336,336]{1,0:T(8,128)} reshape(f32[16,21,16,21]{3,2,1,0:T(8,128)} %mul.99) | data formatting | bytes 903168 | tf_op jit(solution)/shard_map/mul | solution.py:16
  186.0 2.0 select_bitcast_fusion
  188.0 9.4 %mul.110 = f32[4,16,21,16,21]{4,3,2,1,0:T(8,128)} reshape(f32[4,336,336]{2,1,0:T(8,128)} %fusion.14) | data formatting | bytes 3612672 | tf_op jit(solution)/shard_map/mul | solution.py:14
  197.4 4.9 %reduce_sum.29 = f32[4,16,16]{2,1,0:T(8,128)S(1)} reduce(f32[4,16,21,16,21]{4,3,2,1,0:T(8,128)} %mul.110, f32[]{:T(128)} %constant.21.clone.1), dimensions={2,4}, to_apply=%region_8.9 | reduce | flops 450560 | bytes 1810436 | tf_op jit(solution)/shard_map/reduce_sum | solution.py:14
  202.3 5.0 %mul.111 = f32[4,16,21,16,21]{4,3,2,1,0:T(8,128)} broadcast(f32[4,16,16]{2,1,0:T(8,128)S(1)} %subtract_maximum_fusion), dimensions={0,1,3} | broadcast | bytes 1810432 | tf_op jit(solution)/shard_map/mul | solution.py:16
  207.3 9.3 %mul.112 = f32[4,336,336]{2,1,0:T(8,128)} reshape(f32[4,16,21,16,21]{4,3,2,1,0:T(8,128)} %mul.111) | data formatting | bytes 3612672 | tf_op jit(solution)/shard_map/mul | solution.py:16
  216.6 3.8 %multiply_bitcast_fusion = f32[1,4,336,336]{3,2,1,0:T(8,128)} fusion(f32[4,336,336]{2,1,0:T(8,128)} %mul.112, f32[4]{0:T(128)S(1)} %convert_reduce_fusion, f32[4,336,336]{2,1,0:T(8,128)} %get-tuple-element.4, f32[1,4,336,336]{3,2,1,0:T(8,128)S(1)} %copy-done), kind=kLoop, calls=%fused_computation.4 | loop fusion | flops 1806336 | bytes 7225360 | tf_op jit(solution)/shard_map/broadcast_in_dim | solution.py:82
  (40 shorter events, 2.5 us)
Async XLA Ops:
  15.9 7.6 %copy-start.4 = (f32[16,21]{1,0:T(8,128)S(1)}, f32[16,21]{1,0:T(8,128)}, u32[]{:S(2)}) copy-start(f32[16,21]{1,0:T(8,128)} %param.9) | copy-start | bytes 4036
  15.9 7.8 %copy-start.3 = (s32[128,16]{0,1:T(8,128)S(1)}, s32[128,16]{0,1:T(8,128)}, u32[]{:S(2)}) copy-start(s32[128,16]{0,1:T(8,128)} %param.7) | copy-start | bytes 24580
  15.9 8.1 %copy-start.5 = (s32[128]{0:T(128)S(1)}, s32[128]{0:T(128)}, u32[]{:S(2)}) copy-start(s32[128]{0:T(128)} %param.8) | copy-start | bytes 1540
  15.9 36.4 %copy-start.1 = (f32[1,336,336]{2,1,0:T(8,128)S(1)}, f32[1,336,336]{2,1,0:T(8,128)}, u32[]{:S(2)}) copy-start(f32[1,336,336]{2,1,0:T(8,128)} %param.10) | copy-start | bytes 1354756
  15.9 36.1 %all-to-all-start = ((bf16[16,128,336]{1,2,0:T(8,128)(2,1)}), bf16[16,128,336]{1,2,0:T(8,128)(2,1)S(1)}, u32[]{:S(2)}, u32[]{:S(2)}) async-start(bf16[16,128,336]{1,2,0:T(8,128)(2,1)} %copy.37), calls=%async_computation | async-start | bytes 2752512 | tf_op jit(solution)/shard_map/all_to_all | solution.py:49
  54.8 36.8 %all-to-all-start.1 = ((bf16[16,128,336]{1,2,0:T(8,128)(2,1)}), bf16[16,128,336]{1,2,0:T(8,128)(2,1)S(1)}, u32[]{:S(2)}, u32[]{:S(2)}) async-start(bf16[16,128,336]{1,2,0:T(8,128)(2,1)} %broadcast_multiply_fusion), calls=%async_computation.1 | async-start | bytes 2752512 | tf_op jit(solution)/shard_map/all_to_all | solution.py:69
  63.1 108.1 %all-reduce.3.cloned.1.call-start = ((), (), s32[]{:S(2)}) async-start(), calls=%async_computation.2 | async-start | bytes 5160960 | tf_op jit(solution)/shard_map/psum | solution.py:74
  93.7 78.5 %copy-start = (f32[1,4,336,336]{3,2,1,0:T(8,128)S(1)}, f32[1,4,336,336]{3,2,1,0:T(8,128)}, u32[]{:S(2)}) copy-start(f32[1,4,336,336]{3,2,1,0:T(8,128)} %param.11) | copy-start | bytes 5419012
  182.5 3.5 %copy-start.2 = (f32[336,336]{1,0:T(8,128)S(1)}, f32[336,336]{1,0:T(8,128)}, u32[]{:S(2)}) copy-start(f32[336,336]{1,0:T(8,128)} %get-tuple-element.3) | copy-start | bytes 1354756
Sparse Core Ops, SparseCore 0:
  93.9 77.2 all-reduce.2
where the time goes:
time: 228 us; the launch traced here: 227 us
  waiting for transfers between devices  127 us (56%)
  local copies, waits for them, and re-layouts  35 us (15%)
  other arithmetic  23.1 us (10%)
  starting transfers between devices  15.8 us (7%)
  between operations  14.3 us (6%)
  matrix products  7.38 us (3%)
  blocking collectives  5.11 us (2%)
    psum x1, waiting for transfers between devices, per_device(): lax.psum((grad_diag, grad_slots, grad_fields), 'seq')  71.2 us
    all_to_all x1, waiting for transfers between devices, per_device(): lax.all_to_all(outgoing, 'pos', split_axis=0, concat_axis=0, tiled=True)  27.9 us
    all_to_all x1, waiting for transfers between devices, per_device(): lax.all_to_all(sending, 'pos', split_axis=0, concat_axis=0, tiled=True)  27.5 us
    mul x4, local copies, waits for them, and re-layouts, shrink_whole(): return (grouped * factor).reshape(values.shape)  19.6 us
    mul x2, local copies, waits for them, and re-layouts, shrink_whole(): square_sums = jnp.sum(grouped * grouped, axis=(-3, -1), keepdims=True)  12.6 us
    all_to_all x1, starting transfers between devices, per_device(): lax.all_to_all(sending, 'pos', split_axis=0, concat_axis=0, tiled=True)  8.27 us
    all_to_all x1, starting transfers between devices, per_device(): lax.all_to_all(outgoing, 'pos', split_axis=0, concat_axis=0, tiled=True)  7.5 us
    reduce_sum x2, other arithmetic, shrink_whole(): square_sums = jnp.sum(grouped * grouped, axis=(-3, -1), keepdims=True)  6.95 us
  transfers between devices with their start and end apart: 3, of which 3 were waited for; matrix products, arithmetic and copies ran while one was open for 1% of the time, Pallas kernels for 0%

commit v1 on v0

v1 whole, which is shorter than its diff:
```python
import functools
import jax
import jax.numpy as jnp
from jax import lax
from jax.experimental import pallas as pl
from jax.experimental.pallas import tpu as pltpu
from jax.sharding import PartitionSpec as P

STEP_SIZE = 0.2
THRESHOLD = 0.3
HIGHEST_MODE = lax.Precision.HIGHEST
F32 = jnp.float32
BF16 = jnp.bfloat16


def halves(values):
    high = values.astype(BF16)
    return high, (values - high.astype(F32)).astype(BF16)


def times(left, right):
    return jnp.dot(left, right, preferred_element_type=F32)


def indicator(rows, columns, states_count):
    row = lax.broadcasted_iota(jnp.int32, (rows, columns), 0)
    column = lax.broadcasted_iota(jnp.int32, (rows, columns), 1)
    return jnp.where((column >= row * states_count) & (column < (row + 1) * states_count), 1.0, 0.0).astype(BF16)


def indicator_t(rows, columns, states_count):
    row = lax.broadcasted_iota(jnp.int32, (rows, columns), 0)
    column = lax.broadcasted_iota(jnp.int32, (rows, columns), 1)
    return jnp.where((row >= column * states_count) & (row < (column + 1) * states_count), 1.0, 0.0).astype(BF16)


def step_kernel(
    block_len, states_count, slots,
    ids_ref, alive_ref, resid_ref, states_ref, fields_ref, diag_ref, slot_ref,
    new_fields_ref, new_diag_ref, new_slots_ref, onehot_ref,
):
    width = block_len * states_count
    step = pl.program_id(0)
    groups = indicator(block_len, width, states_count)
    groups_t = indicator_t(width, block_len, states_count)

    @pl.when(step == 0)
    def _():
        spread = times(states_ref[...].astype(F32).astype(BF16), groups)
        column = lax.broadcasted_iota(jnp.int32, (1, width), 1)
        start = jnp.zeros((1, width), jnp.int32)
        for p in range(1, block_len):
            start = jnp.where(column >= p * states_count, p * states_count, start)
        onehot_ref[...] = jnp.where(spread == (column - start).astype(F32), 1.0, 0.0).astype(BF16)

    resid = resid_ref[...].reshape(-1, width)
    grad = lax.dot_general(
        resid, onehot_ref[...], (((0,), (0,)), ((), ())), preferred_element_type=F32
    )

    def factors(values):
        high, low = halves(values * values)
        sums = times(groups, high) + times(groups, low)
        high, low = halves(sums)
        sums = times(high, groups_t) + times(low, groups_t)
        factor = jnp.maximum(0.0, 1.0 - THRESHOLD / jnp.sqrt(sums + 1e-06))
        return factor

    def expand(factor):
        high, low = halves(factor)
        wide = times(high, groups) + times(low, groups)
        high, low = halves(wide)
        return times(groups_t, high) + times(groups_t, low)

    @pl.when(step < slots)
    def _():
        values = slot_ref[0, 0] - STEP_SIZE * grad
        keep = alive_ref[step].astype(F32)
        new_slots_ref[0, 0] = values * expand(factors(values) * keep)

    @pl.when(step == slots)
    def _():
        values = diag_ref[0] - STEP_SIZE * grad
        row = lax.broadcasted_iota(jnp.int32, (block_len, block_len), 0)
        column = lax.broadcasted_iota(jnp.int32, (block_len, block_len), 1)
        factor = jnp.where(row == column, 0.0, factors(values))
        new_diag_ref[0] = values * expand(factor)
        ones = jnp.ones((8, resid.shape[0]), BF16)
        new_fields_ref[...] = fields_ref[...] - STEP_SIZE * times(ones, resid)[:1]


def apply_step(ids, alive, gathered, states_all, fields, diag_couplings, slot_couplings):
    seqs, blocks, seq_rows, width = gathered.shape
    slots = slot_couplings.shape[1]
    block_len, states_count = fields.shape
    last = slots - 1
    spec = pltpu.PrefetchScalarGridSpec(
        num_scalar_prefetch=2,
        grid=(slots + 1,),
        in_specs=[
            pl.BlockSpec((seqs, 1, seq_rows, width), lambda i, ids, alive: (0, ids[i], 0, 0)),
            pl.BlockSpec(states_all.shape, lambda i, ids, alive: (0, 0)),
            pl.BlockSpec((1, width), lambda i, ids, alive: (0, 0)),
            pl.BlockSpec((1, width, width), lambda i, ids, alive: (0, 0, 0)),
            pl.BlockSpec((1, 1, width, width), lambda i, ids, alive: (0, jnp.minimum(i, last), 0, 0)),
        ],
        out_specs=[
            pl.BlockSpec((1, width), lambda i, ids, alive: (0, 0)),
            pl.BlockSpec((1, width, width), lambda i, ids, alive: (0, 0, 0)),
            pl.BlockSpec((1, 1, width, width), lambda i, ids, alive: (0, jnp.minimum(i, last), 0, 0)),
        ],
        scratch_shapes=[pltpu.VMEM((states_all.shape[0], width), BF16)],
    )
    new_fields, new_diag, new_slots = pl.pallas_call(
        functools.partial(step_kernel, block_len, states_count, slots),
        grid_spec=spec,
        out_shape=[
            jax.ShapeDtypeStruct((1, width), F32),
            jax.ShapeDtypeStruct(diag_couplings.shape, F32),
            jax.ShapeDtypeStruct(slot_couplings.shape, F32),
        ],
        compiler_params=pltpu.CompilerParams(vmem_limit_bytes=40 * 1024 * 1024),
    )(ids, alive, gathered, states_all, fields.reshape(1, width), diag_couplings, slot_couplings)
    return new_fields.reshape(block_len, states_count), new_diag, new_slots


def per_device(
    states, multiplicity, fields, diag_couplings, slot_couplings, slot_blocks, partner_blocks
):
    seq_rows, block_len = states.shape
    states_count = fields.shape[1]
    row_width = block_len * states_count
    blocks = lax.axis_size("pos")
    my_block = lax.axis_index("pos")
    states_all = lax.all_gather(states, "seq", axis=0, tiled=True)
    onehot_wide = jax.nn.one_hot(states, states_count, dtype=F32).reshape(seq_rows, row_width)
    weight = 1.0 / multiplicity.astype(F32)
    position = jnp.arange(row_width) // states_count
    off_self = (position[:, None] != position[None, :]).astype(F32)
    my_slots = lax.dynamic_index_in_dim(slot_blocks, my_block, axis=0, keepdims=False)
    row_ids = jnp.maximum(my_slots, 0)
    partners = jnp.take(partner_blocks, row_ids, axis=0)
    alive = (my_slots >= 0) & jnp.any(partners == my_block, axis=1)
    block_ids = jnp.arange(blocks, dtype=jnp.int32)
    slot_pick = ((my_slots[:, None] == block_ids[None, :]) & alive[:, None]).astype(BF16)
    slot_terms = jnp.einsum(
        "nk,tik->tni", onehot_wide, slot_couplings[0], precision=HIGHEST_MODE
    ).astype(BF16)
    outgoing = jnp.einsum("td,tnk->dnk", slot_pick, slot_terms, preferred_element_type=BF16)
    arrived = lax.all_to_all(outgoing, "pos", split_axis=0, concat_axis=0, tiled=True)
    source_ones = jnp.ones((arrived.shape[0],), BF16)
    incoming = jnp.einsum("d,dnk->nk", source_ones, arrived, preferred_element_type=F32)
    own_terms = jnp.einsum(
        "nk,ik->ni", onehot_wide, diag_couplings[0] * off_self, precision=HIGHEST_MODE
    )
    logits = fields.reshape(1, row_width) + own_terms + incoming
    probabilities = jax.nn.softmax(
        logits.reshape(seq_rows, block_len, states_count), axis=-1
    ).reshape(seq_rows, row_width)
    residual = (weight[:, None] * (probabilities - onehot_wide)).astype(BF16)
    block_resid = lax.all_gather(residual, "pos", axis=0, tiled=False)
    ids = jnp.concatenate([row_ids, my_block[None].astype(jnp.int32)])
    wanted = jnp.concatenate(
        [lax.dynamic_index_in_dim(block_resid, ids[t], axis=0) for t in range(ids.shape[0])]
    )
    gathered = lax.all_gather(wanted, "seq", axis=0, tiled=False)
    ids = jnp.arange(ids.shape[0], dtype=jnp.int32)
    return apply_step(
        ids, alive.astype(jnp.int32), gathered, states_all, fields, diag_couplings, slot_couplings
    )


def solution(mesh):
    placed = (
        P("seq", "pos"),
        P("seq"),
        P("pos", None),
        P("pos", None, None),
        P("pos", None, None, None),
        P(),
        P(),
    )
    return jax.shard_map(
        per_device,
        mesh=mesh,
        in_specs=placed,
        out_specs=(P("pos", None), P("pos", None, None), P("pos", None, None, None)),
        check_vma=False,
    )
```

time: 228 us -> 130 us (0.57)
  waiting for transfers between devices: 127 us -> 56.1 us
  local copies, waits for them, and re-layouts: 35 us -> 9.89 us
  other arithmetic: 23.1 us -> 3.19 us
  blocking collectives: 5.11 us -> 18.4 us
  starting transfers between devices: 15.8 us -> 7.53 us
  Pallas kernels: 0 us -> 8.06 us
  between operations: 14.3 us -> 22 us
  matrix products: 7.38 us -> 4.05 us
    psum x1 -> x0, waiting for transfers between devices: 71.2 us -> none  [per_device(): lax.psum((grad_diag, grad_slots, grad_fields), 'seq')]
    mul x6 -> x0, local copies, waits for them, and re-layouts: 32.3 us -> none  [the longest x4 19.6 us: shrink_whole(): return (grouped * factor).reshape(values.shape)]
    all_gather x0 -> x1, waiting for transfers between devices: none -> 27.9 us  [per_device(): block_resid = lax.all_gather(residual, 'pos', axis=0, tiled=False)]
    all_to_all x1 -> x0, waiting for transfers between devices: 27.5 us -> none  [per_device(): lax.all_to_all(sending, 'pos', split_axis=0, concat_axis=0, tiled=True)]
    all_gather x0 -> x2, blocking collectives: none -> 18.4 us  [the longest x1 13 us: per_device(): gathered = lax.all_gather(wanted, 'seq', axis=0, tiled=False)]
    all_to_all x1 -> x0, starting transfers between devices: 8.27 us -> none  [per_device(): lax.all_to_all(sending, 'pos', split_axis=0, concat_axis=0, tiled=True)]
    pallas_call x0 -> x1, Pallas kernels: none -> 8.06 us  [apply_step(): pl.pallas_call(functools.partial(step_kernel, block_len, states_count, sl...]
    reduce_sum x2 -> x0, other arithmetic: 6.95 us -> none  [shrink_whole(): square_sums = jnp.sum(grouped * grouped, axis=(-3, -1), keepdims=True)]
  transfers between devices with their start and end apart: 3 -> 2, of which waited for: 3 -> 2; matrix products, arithmetic and copies ran while one was open for 1% -> 1% of each run, Pallas kernels for 0% -> 0%
where the time goes in v1:
time: 130 us; the launch traced here: 129 us
  waiting for transfers between devices  56.1 us (43%)
  between operations  22 us (17%)
  blocking collectives  18.4 us (14%)
  local copies, waits for them, and re-layouts  9.89 us (8%)
  Pallas kernels  8.06 us (6%)
  starting transfers between devices  7.53 us (6%)
  matrix products  4.05 us (3%)
  other arithmetic  3.19 us (2%)
    all_to_all x1, waiting for transfers between devices, per_device(): lax.all_to_all(outgoing, 'pos', split_axis=0, concat_axis=0, tiled=True)  28.1 us
    all_gather x1, waiting for transfers between devices, per_device(): block_resid = lax.all_gather(residual, 'pos', axis=0, tiled=False)  27.9 us
    all_gather x1, blocking collectives, per_device(): gathered = lax.all_gather(wanted, 'seq', axis=0, tiled=False)  13 us
    pallas_call x1, Pallas kernels, apply_step(): pl.pallas_call(functools.partial(step_kernel, block_len, states_count, sl...  8.06 us
    all_to_all x1, starting transfers between devices, per_device(): lax.all_to_all(outgoing, 'pos', split_axis=0, concat_axis=0, tiled=True)  7.49 us
    all_gather x1, blocking collectives, per_device(): states_all = lax.all_gather(states, 'seq', axis=0, tiled=True)  5.45 us
    unnamed x19, local copies, waits for them, and re-layouts  3.66 us
  transfers between devices with their start and end apart: 2, of which 2 were waited for; matrix products, arithmetic and copies ran while one was open for 1% of the time, Pallas kernels for 0%

profile of v1, /device:TPU:0, one launch (start us, length us, event | category | flops | bytes accessed | tf_op | source)
XLA Modules:
  0.0 129.3 jit_solution(1472179781081151546)
XLA Ops:
  7.2 0.9 dynamic-slice_reduce_fusion
  8.1 0.8 copy.24
  8.9 0.6 gather_fusion
  9.4 0.2 fusion.26
  9.6 0.7 iota_compare_fusion
  10.4 2.6 %fusion.8 = bf16[4,128,336]{1,2,0:T(8,128)(2,1)S(1)} fusion(pred[128,336,1]{0,1,2:T(8,128)(4,1)S(1)} %reshape.195, f32[1,4,336,336]{3,2,1,0:T(8,128)} %slot_ref.1), kind=kOutput, calls=%fused_computation.7 | convolution fusion | flops 693805056 | bytes 2193408 | tf_op jit(solution)/shard_map/nk,tik->tni/dot_general | solution.py:146
  13.0 0.7 fusion.15
  13.7 1.4 %copy.26 = bf16[16,128,336]{1,2,0:T(8,128)(2,1)} copy(bf16[16,128,336]{1,0,2:T(8,128)(2,1)S(1)} %fusion.15) | data formatting | bytes 2752512 | tf_op jit(solution)/shard_map/td,tnk->dnk/dot_general | solution.py:149
  15.1 7.5 %all-to-all-start = ((bf16[16,128,336]{1,2,0:T(8,128)(2,1)}), bf16[16,128,336]{1,2,0:T(8,128)(2,1)S(1)}, u32[]{:S(2)}, u32[]{:S(2)}) async-start(bf16[16,128,336]{1,2,0:T(8,128)(2,1)} %copy.26), calls=%async_computation | async-start | bytes 2752512 | tf_op jit(solution)/shard_map/all_to_all | solution.py:150
  22.6 0.0 copy-start.1
  22.6 0.0 all-gather.4.cloned.1.call-start
  22.7 0.1 add.43
  22.8 0.1 eq.75
  23.0 28.1 %all-to-all-done = bf16[16,128,336]{1,2,0:T(8,128)(2,1)S(1)} async-done(((bf16[16,128,336]{1,2,0:T(8,128)(2,1)}), bf16[16,128,336]{1,2,0:T(8,128)(2,1)S(1)}, u32[]{:S(2)}, u32[]{:S(2)}) %all-to-all-start) | async-done | bytes 1376288 | tf_op jit(solution)/shard_map/all_to_all | solution.py:150
  51.2 0.4 fusion.3
  51.5 0.4 fusion.11
  52.0 0.5 fusion
  52.6 0.8 multiply_convert_fusion
  53.4 0.0 all-gather.4.cloned.1.call-update
  53.4 0.1 reshape.182.fields_ref
  53.5 0.6 fusion.36
  59.3 0.1 copy.33
  61.9 5.4 %all_gather.19.states_ref = s32[256,16]{1,0:T(8,128)S(1)} all-gather(s32[128,16]{1,0:T(8,128)S(1)} %copy.33), channel_id=1, replica_groups=mesh['seq'=2,'pos'=16] {'seq'}, dimensions={0}, use_global_device_ids=true | all-gather | bytes 24576 | tf_op jit(solution)/shard_map/all_gather | solution.py:135
  67.4 27.9 %all-gather.4.cloned.1.call-done = bf16[2048,336]{0,1:T(8,128)(2,1)} async-done(((bf16[128,336]{0,1:T(8,128)(2,1)}), bf16[2048,336]{0,1:T(8,128)(2,1)}) %all-gather.4.cloned.1.call-update) | async-done | bytes 1376272 | tf_op jit(solution)/shard_map/all_gather | solution.py:161
  95.3 1.7 %copy.41 = bf16[42,8,16,128]{3,2,1,0:T(8,128)(2,1)S(1)} copy(bf16[42,8,16,128]{3,1,2,0:T(8,128)(2,1)} %bitcast.43) | data formatting | bytes 2752512
  97.0 0.9 constant_dynamic-slice_fusion
  98.0 0.0 copy-start
  98.0 13.0 %all-gather.1 = bf16[10,128,336]{1,2,0:T(8,128)(2,1)} all-gather(bf16[5,128,336]{1,2,0:T(8,128)(2,1)S(1)} %copy_dynamic-update-slice_fusion), channel_id=3, replica_groups=mesh['seq'=2,'pos'=16] {'seq'}, dimensions={0}, use_global_device_ids=true | all-gather | bytes 1290240 | tf_op jit(solution)/shard_map/all_gather | solution.py:166
  111.0 1.6 %copy.32 = bf16[10,128,336]{2,1,0:T(8,128)(2,1)S(1)} copy(bf16[10,128,336]{1,2,0:T(8,128)(2,1)} %all-gather.1) | data formatting | bytes 1720320 | tf_op jit(solution)/shard_map/all_gather | solution.py:166
  112.6 1.0 copy-done.2
  113.7 8.1 %shard_map.94 = (f32[1,336]{1,0:T(1,128)S(1)}, f32[1,336,336]{2,1,0:T(8,128)}, f32[1,4,336,336]{3,2,1,0:T(8,128)}) custom-call(s32[5]{0:T(128)S(1)} %iota.36.ids_ref, s32[4]{0:T(128)S(1)} %get-tuple-element.11.alive_ref, bf16[2,5,128,336]{3,2,1,0:T(8,128)(2,1)S(1)} %bitcast.41, s32[256,16]{1,0:T(8,128)S(1)} %all_gather.19.states_ref, ...), custom_call_target="tpu_custom_call" | custom-call | tf_op jit(solution)/shard_map/pallas_call | solution.py:114
  121.7 0.7 reshape.183
  (32 shorter events, 0.4 us)
Async XLA Ops:
  15.1 7.6 %copy-start.4 = (f32[16,21]{1,0:T(8,128)S(1)}, f32[16,21]{1,0:T(8,128)}, u32[]{:S(2)}) copy-start(f32[16,21]{1,0:T(8,128)} %param.9) | copy-start | bytes 4036
  15.1 7.8 %copy-start.3 = (s32[128,16]{0,1:T(8,128)S(1)}, s32[128,16]{0,1:T(8,128)}, u32[]{:S(2)}) copy-start(s32[128,16]{0,1:T(8,128)} %param.7) | copy-start | bytes 24580
  15.1 7.9 %copy-start.5 = (s32[128]{0:T(128)S(1)}, s32[128]{0:T(128)}, u32[]{:S(2)}) copy-start(s32[128]{0:T(128)} %param.8) | copy-start | bytes 1540
  15.1 36.1 %all-to-all-start = ((bf16[16,128,336]{1,2,0:T(8,128)(2,1)}), bf16[16,128,336]{1,2,0:T(8,128)(2,1)S(1)}, u32[]{:S(2)}, u32[]{:S(2)}) async-start(bf16[16,128,336]{1,2,0:T(8,128)(2,1)} %copy.26), calls=%async_computation | async-start | bytes 2752512 | tf_op jit(solution)/shard_map/all_to_all | solution.py:150
  22.6 28.9 %copy-start.1 = (f32[1,336,336]{2,1,0:T(8,128)S(1)}, f32[1,336,336]{2,1,0:T(8,128)}, u32[]{:S(2)}) copy-start(f32[1,336,336]{2,1,0:T(8,128)} %diag_ref.1) | copy-start | bytes 1354756
  22.6 72.7 %all-gather.4.cloned.1.call-start = ((), (), s32[]{:S(2)}) async-start(), calls=%async_computation.1 | async-start | bytes 1462272 | tf_op jit(solution)/shard_map/all_gather | solution.py:161
  98.0 14.6 %copy-start = (f32[1,4,336,336]{3,2,1,0:T(8,128)S(1)}, f32[1,4,336,336]{3,2,1,0:T(8,128)}, u32[]{:S(2)}) copy-start(f32[1,4,336,336]{3,2,1,0:T(8,128)} %slot_ref.1) | copy-start | bytes 5419012
  112.6 1.0 copy-start.2
Sparse Core Ops, SparseCore 0:
  53.5 41.7 all-gather.3

commit v2 on v1

v2 whole, which is shorter than its diff:
```python
import functools
import jax
import jax.numpy as jnp
from jax import lax
from jax.experimental import pallas as pl
from jax.experimental.pallas import tpu as pltpu
from jax.sharding import PartitionSpec as P

STEP_SIZE = 0.2
THRESHOLD = 0.3
F32 = jnp.float32
BF16 = jnp.bfloat16


def halves(values):
    high = values.astype(BF16)
    return high, (values - high.astype(F32)).astype(BF16)


def times(left, right):
    return jnp.dot(left, right, preferred_element_type=F32)


def indicator(rows, columns, states_count):
    row = lax.broadcasted_iota(jnp.int32, (rows, columns), 0)
    column = lax.broadcasted_iota(jnp.int32, (rows, columns), 1)
    return jnp.where((column >= row * states_count) & (column < (row + 1) * states_count), 1.0, 0.0).astype(BF16)


def indicator_t(rows, columns, states_count):
    row = lax.broadcasted_iota(jnp.int32, (rows, columns), 0)
    column = lax.broadcasted_iota(jnp.int32, (rows, columns), 1)
    return jnp.where((row >= column * states_count) & (row < (column + 1) * states_count), 1.0, 0.0).astype(BF16)


def position_starts(block_len, states_count):
    column = lax.broadcasted_iota(jnp.int32, (1, block_len * states_count), 1)
    start = jnp.zeros_like(column)
    for p in range(1, block_len):
        start = jnp.where(column >= p * states_count, p * states_count, start)
    return column, start


def onehot_of(states_t, groups, column, start):
    spread = lax.dot_general(
        states_t, groups, (((0,), (0,)), ((), ())), preferred_element_type=F32
    )
    return jnp.where(spread == (column - start).astype(F32), 1.0, 0.0).astype(BF16)


def exchange_kernel(
    block_len, states_count, seqs, highs, lows,
    slot_blocks_ref, partner_ref, states_ref, multiplicity_ref, fields_ref, diag_ref, slot_ref,
    out_ref, states_out_ref,
    term_ref, near_ref, high1_ref, stage1_ref, low1_ref, high2_ref, stage2_ref, low2_ref,
    send_sem, recv_sem,
):
    width = block_len * states_count
    slots = slot_ref.shape[1]
    far = slots - 2
    blocks = highs * lows
    seq = lax.axis_index("seq")
    pos = lax.axis_index("pos")
    high = pos // lows
    low = pos % lows

    def place(f, target):
        return (lax.rem(seq + f, seqs), target)

    def beside(g):
        return lax.rem(pos + g + blocks, blocks)

    def high_peer(d):
        return lax.rem(high + d, highs) * lows + low

    def low_peer(e):
        return high * lows + lax.rem(low + e, lows)

    near = [(f, g) for g in (0, 1, -1) for f in range(seqs) if (f, g) != (0, 0)]
    peers = [place(f, beside(g)) for f, g in near]
    peers += [place(0, high_peer(d)) for d in range(1, highs)]
    peers += [place(0, low_peer(e)) for e in range(1, lows)]
    barrier = pltpu.get_barrier_semaphore()
    for peer in peers:
        pl.semaphore_signal(barrier, inc=1, device_id=peer, device_id_type=pl.DeviceIdType.MESH)

    groups = indicator(block_len, width, states_count)
    column, start = position_starts(block_len, states_count)
    onehot = onehot_of(states_ref[...], groups, column, start)

    def terms(values):
        first = values.astype(BF16)
        rest = values - first.astype(F32)
        second = rest.astype(BF16)
        third = (rest - second.astype(F32)).astype(BF16)
        total = None
        for part in (third, second, first):
            product = lax.dot_general(
                onehot, part, (((1,), (1,)), ((), ())), preferred_element_type=F32
            )
            total = product if total is None else total + product
        return total

    copies = []

    def send(source, target, device):
        k = len(copies)
        copy = pltpu.make_async_remote_copy(
            src_ref=source, dst_ref=target, send_sem=send_sem.at[k], recv_sem=recv_sem.at[k],
            device_id=device, device_id_type=pl.DeviceIdType.MESH,
        )
        copy.start()
        copies.append(copy)
        return copy

    for t in range(far):
        high1_ref[0, t] = terms(slot_ref[0, 2 + t]).astype(BF16)
    states_out_ref[0] = states_ref[...]
    pl.semaphore_wait(barrier, len(peers))
    high1 = [
        send(high1_ref.at[0], high1_ref.at[d], place(0, high_peer(d))) for d in range(1, highs)
    ]
    for t in range(2):
        term_ref[t] = terms(slot_ref[0, t]).astype(BF16)
    near1 = [
        send(term_ref.at[0], near_ref.at[0], place(0, beside(-1))),
        send(term_ref.at[1], near_ref.at[1], place(0, beside(1))),
    ]
    states_moves = [
        send(states_ref, states_out_ref.at[f], place(f, pos)) for f in range(1, seqs)
    ]
    mask = jnp.zeros((width, width), jnp.bool_)
    row = lax.broadcasted_iota(jnp.int32, (width, width), 0)
    wide = lax.broadcasted_iota(jnp.int32, (width, width), 1)
    for p in range(block_len):
        lo, hi = p * states_count, (p + 1) * states_count
        mask = mask | ((row >= lo) & (row < hi) & (wide >= lo) & (wide < hi))
    logits = fields_ref[...] + terms(jnp.where(mask, 0.0, diag_ref[0]))
    same = jnp.where(mask, 1.0, 0.0).astype(BF16)

    def search(target, t):
        def one(c, found):
            return jnp.where(slot_blocks_ref[c, t] == target, c, found)

        return lax.fori_loop(0, blocks, one, jnp.int32(-1))

    def listed(holder):
        hit = partner_ref[pos, 0] == holder
        for k in range(1, slots):
            hit = hit | (partner_ref[pos, k] == holder)
        return jnp.where(hit & (holder >= 0), 1.0, 0.0).astype(F32)

    holders = [search(pos, t) for t in range(slots)]

    def ring(value, size):
        return lax.rem(value + size, size)

    for copy in high1:
        copy.wait_recv()
    low1 = []
    for e in list(range(1, lows)) + [0]:
        for t in range(far):
            target = low_peer(e)
            pick = jnp.int32(0)
            for h in range(highs):
                found = slot_blocks_ref[h * lows + low, 2 + t] == target
                pick = jnp.where(found, ring(high - h, highs), pick)
            value = high1_ref[pick, t]
            if e == 0:
                low1_ref[0, t] = value
            else:
                stage1_ref[e, t] = value
        if e:
            low1.append(send(stage1_ref.at[e], low1_ref.at[e], place(0, target)))
    for copy in near1:
        copy.wait_recv()
    incoming = near_ref[0].astype(F32) * listed(holders[0])
    incoming += near_ref[1].astype(F32) * listed(holders[1])
    for copy in low1:
        copy.wait_recv()
    for t in range(far):
        holder = holders[2 + t]
        pick = ring(low - lax.rem(jnp.maximum(holder, 0), lows), lows)
        incoming += low1_ref[pick, t].astype(F32) * listed(holder)
    logits += incoming

    peak = jnp.zeros_like(logits)
    for p in range(block_len):
        inside = start == p * states_count
        top = jnp.max(jnp.where(inside, logits, -jnp.inf), axis=1, keepdims=True)
        peak = jnp.where(inside, top, peak)
    powers = jnp.exp(logits - peak)
    first, second = halves(powers)
    probabilities = powers / (times(first, same) + times(second, same))
    weight = 1.0 / multiplicity_ref[...]
    residual = (weight * (probabilities - onehot.astype(F32))).astype(BF16)
    high2_ref[0] = residual
    out_ref[0, slots] = residual

    high2 = [
        send(high2_ref.at[0], high2_ref.at[d], place(0, high_peer(d))) for d in range(1, highs)
    ]
    slot_of = {0: slots, 1: 0, -1: 1}
    last = [
        send(high2_ref.at[0], out_ref.at[f, slot_of[g]], place(f, beside(g))) for f, g in near
    ]
    for copy in high2:
        copy.wait_recv()
    low2 = []
    for e in list(range(1, lows)) + [0]:
        for t in range(far):
            target = low_peer(e)
            wanted = jnp.maximum(slot_blocks_ref[target, 2 + t], 0)
            value = high2_ref[ring(high - wanted // lows, highs)]
            if e == 0:
                low2_ref[0, t] = value
            else:
                stage2_ref[e, t] = value
        if e:
            low2.append(send(stage2_ref.at[e], low2_ref.at[e], place(0, target)))
    for copy in low2:
        copy.wait_recv()
    for t in range(far):
        wanted = jnp.maximum(slot_blocks_ref[pos, 2 + t], 0)
        out_ref[0, 2 + t] = low2_ref[ring(low - lax.rem(wanted, lows), lows), t]
    last += [
        send(out_ref.at[0, pl.ds(2, far)], out_ref.at[f, pl.ds(2, far)], place(f, pos))
        for f in range(1, seqs)
    ]
    for copy in states_moves + last:
        copy.wait_recv()
    for copy in copies:
        copy.wait_send()


def exchange(slot_blocks, partner_blocks, states_t, multiplicity, fields, diag, slot):
    block_len, seq_rows = states_t.shape
    width = fields.shape[1]
    slots = slot.shape[1]
    seqs, blocks = lax.axis_size("seq"), lax.axis_size("pos")
    lows = 4 if blocks % 4 == 0 else 1
    highs = blocks // lows
    moves = 2 * (highs - 1) + 2 * (lows - 1) + 2 + (seqs - 1) * 2 + 3 * seqs
    vmem = pl.BlockSpec(memory_space=pltpu.VMEM)
    smem = pl.BlockSpec(memory_space=pltpu.SMEM)
    far = slots - 2
    tile = (seq_rows, width)
    return pl.pallas_call(
        functools.partial(exchange_kernel, block_len, width // block_len, seqs, highs, lows),
        in_specs=[smem, smem, vmem, vmem, vmem, vmem, vmem],
        out_specs=[vmem, vmem],
        out_shape=[
            jax.ShapeDtypeStruct((seqs, slots + 1) + tile, BF16),
            jax.ShapeDtypeStruct((seqs, block_len, seq_rows), BF16),
        ],
        scratch_shapes=[
            pltpu.VMEM((2,) + tile, BF16),
            pltpu.VMEM((2,) + tile, BF16),
            pltpu.VMEM((highs, far) + tile, BF16),
            pltpu.VMEM((lows, far) + tile, BF16),
            pltpu.VMEM((lows, far) + tile, BF16),
            pltpu.VMEM((highs,) + tile, BF16),
            pltpu.VMEM((lows, far) + tile, BF16),
            pltpu.VMEM((lows, far) + tile, BF16),
            pltpu.SemaphoreType.DMA((moves,)),
            pltpu.SemaphoreType.DMA((moves,)),
        ],
        compiler_params=pltpu.CompilerParams(
            collective_id=0, has_side_effects=True, vmem_limit_bytes=48 * 1024 * 1024
        ),
    )(slot_blocks, partner_blocks, states_t, multiplicity, fields, diag, slot)


def step_kernel(
    block_len, states_count, slots,
    slot_blocks_ref, partner_ref, resid_ref, states_ref, fields_ref, diag_ref, slot_ref,
    new_fields_ref, new_diag_ref, new_slots_ref, onehot_ref,
):
    width = block_len * states_count
    step = pl.program_id(0)
    groups = indicator(block_len, width, states_count)
    groups_t = indicator_t(width, block_len, states_count)

    @pl.when(step == 0)
    def _():
        column, start = position_starts(block_len, states_count)
        seq_rows = states_ref.shape[2]
        for f in range(states_ref.shape[0]):
            onehot_ref[pl.ds(f * seq_rows, seq_rows)] = onehot_of(
                states_ref[f], groups, column, start
            )

    resid = resid_ref[...].reshape(-1, width)
    grad = lax.dot_general(
        resid, onehot_ref[...], (((0,), (0,)), ((), ())), preferred_element_type=F32
    )

    def factors(values):
        high, low = halves(values * values)
        sums = times(groups, high) + times(groups, low)
        high, low = halves(sums)
        sums = times(high, groups_t) + times(low, groups_t)
        factor = jnp.maximum(0.0, 1.0 - THRESHOLD / jnp.sqrt(sums + 1e-06))
        return factor

    def expand(factor):
        high, low = halves(factor)
        wide = times(high, groups) + times(low, groups)
        high, low = halves(wide)
        return times(groups_t, high) + times(groups_t, low)

    @pl.when(step < slots)
    def _():
        values = slot_ref[0, 0] - STEP_SIZE * grad
        me = lax.axis_index("pos")
        holder = slot_blocks_ref[me, step]
        listing = jnp.maximum(holder, 0)
        hit = partner_ref[listing, 0] == me
        for k in range(1, slots):
            hit = hit | (partner_ref[listing, k] == me)
        keep = jnp.where(hit & (holder >= 0), 1.0, 0.0).astype(F32)
        new_slots_ref[0, 0] = values * expand(factors(values) * keep)

    @pl.when(step == slots)
    def _():
        values = diag_ref[0] - STEP_SIZE * grad
        row = lax.broadcasted_iota(jnp.int32, (block_len, block_len), 0)
        column = lax.broadcasted_iota(jnp.int32, (block_len, block_len), 1)
        factor = jnp.where(row == column, 0.0, factors(values))
        new_diag_ref[0] = values * expand(factor)
        ones = jnp.ones((8, resid.shape[0]), BF16)
        new_fields_ref[...] = fields_ref[...] - STEP_SIZE * times(ones, resid)[:1]


def apply_step(slot_blocks, partner_blocks, gathered, states_all, fields, diag_couplings, slot_couplings):
    seqs, _, seq_rows, width = gathered.shape
    slots = slot_couplings.shape[1]
    block_len = states_all.shape[1]
    states_count = width // block_len
    last = slots - 1
    spec = pltpu.PrefetchScalarGridSpec(
        num_scalar_prefetch=2,
        grid=(slots + 1,),
        in_specs=[
            pl.BlockSpec((seqs, 1, seq_rows, width), lambda i, ids, alive: (0, i, 0, 0)),
            pl.BlockSpec(states_all.shape, lambda i, ids, alive: (0, 0, 0)),
            pl.BlockSpec((1, width), lambda i, ids, alive: (0, 0)),
            pl.BlockSpec((1, width, width), lambda i, ids, alive: (0, 0, 0)),
            pl.BlockSpec((1, 1, width, width), lambda i, ids, alive: (0, jnp.minimum(i, last), 0, 0)),
        ],
        out_specs=[
            pl.BlockSpec((1, width), lambda i, ids, alive: (0, 0)),
            pl.BlockSpec((1, width, width), lambda i, ids, alive: (0, 0, 0)),
            pl.BlockSpec((1, 1, width, width), lambda i, ids, alive: (0, jnp.minimum(i, last), 0, 0)),
        ],
        scratch_shapes=[pltpu.VMEM((seqs * seq_rows, width), BF16)],
    )
    new_fields, new_diag, new_slots = pl.pallas_call(
        functools.partial(step_kernel, block_len, states_count, slots),
        grid_spec=spec,
        out_shape=[
            jax.ShapeDtypeStruct((1, width), F32),
            jax.ShapeDtypeStruct(diag_couplings.shape, F32),
            jax.ShapeDtypeStruct(slot_couplings.shape, F32),
        ],
        compiler_params=pltpu.CompilerParams(vmem_limit_bytes=40 * 1024 * 1024),
    )(slot_blocks, partner_blocks, gathered, states_all, fields, diag_couplings, slot_couplings)
    return new_fields.reshape(block_len, states_count), new_diag, new_slots


def per_device(
    states, multiplicity, fields, diag_couplings, slot_couplings, slot_blocks, partner_blocks
):
    fields_row = fields.reshape(1, -1)
    gathered, states_all = exchange(
        slot_blocks,
        partner_blocks,
        states.T.astype(BF16),
        multiplicity.astype(F32)[:, None],
        fields_row,
        diag_couplings,
        slot_couplings,
    )
    return apply_step(
        slot_blocks, partner_blocks, gathered, states_all, fields_row, diag_couplings, slot_couplings
    )


def solution(mesh):
    placed = (
        P("seq", "pos"),
        P("seq"),
        P("pos", None),
        P("pos", None, None),
        P("pos", None, None, None),
        P(),
        P(),
    )
    return jax.shard_map(
        per_device,
        mesh=mesh,
        in_specs=placed,
        out_specs=(P("pos", None), P("pos", None, None), P("pos", None, None, None)),
        check_vma=False,
    )
```

time: 130 us -> 72.7 us (0.56)
  the two profiles are of different devices: /device:TPU:0 before, /device:TPU:27 now
where the time goes in v2:
time: 72.7 us; the launch traced here: 72.3 us
  Pallas kernels  64.6 us (89%)
  local copies, waits for them, and re-layouts  5.71 us (8%)
  other arithmetic  1.38 us (2%)
    pallas_call x1, Pallas kernels, exchange(): pl.pallas_call(functools.partial(exchange_kernel, block_len, width // blo...  56.2 us
    pallas_call x1, Pallas kernels, apply_step(): pl.pallas_call(functools.partial(step_kernel, block_len, states_count, sl...  8.37 us
    unnamed x6, local copies, waits for them, and re-layouts  4.13 us

profile of v2, /device:TPU:27, one launch (start us, length us, event | category | flops | bytes accessed | tf_op | source)
XLA Modules:
  0.0 72.3 jit_solution(2820284618308552861)
XLA Ops:
  0.6 0.7 convert_bitcast_fusion.1
  1.3 0.8 %reshape.12.fields_ref = f32[1,336]{1,0:T(1,128)S(1)} reshape(f32[16,21]{1,0:T(8,128)} %param.9) | data formatting | bytes 2688 | tf_op jit(solution)/shard_map/reshape | solution.py:374
  2.1 0.7 convert_bitcast_fusion.states_ref
  2.8 0.8 %copy.13.slot_blocks_ref = s32[16,4]{1,0:T(8,128)S(1)} copy(s32[16,4]{0,1:T(4,128)} %param.12) | data formatting | bytes 512 | tf_op args[5]
  3.5 0.8 %copy.14.partner_ref = s32[16,4]{1,0:T(8,128)S(1)} copy(s32[16,4]{0,1:T(4,128)} %param.13) | data formatting | bytes 512 | tf_op args[6]
  4.3 0.1 copy.12.multiplicity_ref
  4.4 0.0 copy-start
  4.4 1.6 %copy-done = f32[1,4,336,336]{3,2,1,0:T(8,128)S(1)} copy-done((f32[1,4,336,336]{3,2,1,0:T(8,128)S(1)}, f32[1,4,336,336]{3,2,1,0:T(8,128)}, u32[]{:S(2)}) %copy-start) | copy-done | bytes 1806360
  6.0 0.0 copy-start.1
  6.0 1.0 %copy-done.1 = f32[1,336,336]{2,1,0:T(8,128)S(1)} copy-done((f32[1,336,336]{2,1,0:T(8,128)S(1)}, f32[1,336,336]{2,1,0:T(8,128)}, u32[]{:S(2)}) %copy-start.1) | copy-done | bytes 451608
  7.0 56.2 %shard_map.94 = (bf16[2,5,128,336]{3,2,1,0:T(8,128)(2,1)S(1)}, bf16[2,16,128]{2,1,0:T(8,128)(2,1)S(1)}) custom-call(s32[16,4]{1,0:T(8,128)S(1)} %copy.13.slot_blocks_ref, s32[16,4]{1,0:T(8,128)S(1)} %copy.14.partner_ref, bf16[16,128]{1,0:T(8,128)(2,1)S(1)} %convert_bitcast_fusion.states_ref, f32[128,1]{1,0:T(8,128)S(1)} %copy.12.multiplicity_ref, ...), custom_call_target="tpu_custom_call" | custom-call | tf_op jit(solution)/shard_map/pallas_call | solution.py:248
  63.2 8.4 %shard_map.95 = (f32[1,336]{1,0:T(1,128)S(1)}, f32[1,336,336]{2,1,0:T(8,128)}, f32[1,4,336,336]{3,2,1,0:T(8,128)}) custom-call(s32[16,4]{1,0:T(8,128)S(1)} %copy.13.slot_blocks_ref, s32[16,4]{1,0:T(8,128)S(1)} %copy.14.partner_ref, bf16[2,5,128,336]{3,2,1,0:T(8,128)(2,1)S(1)} %get-tuple-element.8.resid_ref, ...), custom_call_target="tpu_custom_call" | custom-call | tf_op jit(solution)/shard_map/pallas_call | solution.py:358
  71.6 0.7 reshape.13
  (1 shorter events, 0.0 us)
Async XLA Ops:
  4.4 1.6 %copy-start = (f32[1,4,336,336]{3,2,1,0:T(8,128)S(1)}, f32[1,4,336,336]{3,2,1,0:T(8,128)}, u32[]{:S(2)}) copy-start(f32[1,4,336,336]{3,2,1,0:T(8,128)} %slot_ref.3) | copy-start | bytes 5419012
  6.0 1.0 %copy-start.1 = (f32[1,336,336]{2,1,0:T(8,128)S(1)}, f32[1,336,336]{2,1,0:T(8,128)}, u32[]{:S(2)}) copy-start(f32[1,336,336]{2,1,0:T(8,128)} %diag_ref.3) | copy-start | bytes 1354756

commit v3 on v2

--- a/solution.py
+++ b/solution.py
@@ -53,7 +53,7 @@
     slot_blocks_ref, partner_ref, states_ref, multiplicity_ref, fields_ref, diag_ref, slot_ref,
     out_ref, states_out_ref,
     term_ref, near_ref, high1_ref, stage1_ref, low1_ref, high2_ref, stage2_ref, low2_ref,
-    send_sem, recv_sem,
+    logits_ref, send_sem, recv_sem,
 ):
     width = block_len * states_count
     slots = slot_ref.shape[1]
@@ -113,12 +113,23 @@
         copies.append(copy)
         return copy
 
+    rows = states_ref.shape[1]
+    chunks = len(high1_ref)
+    depth = rows // chunks
+    parts = [pl.ds(r * depth, depth) for r in range(chunks)]
+
     for t in range(far):
-        high1_ref[0, t] = terms(slot_ref[0, 2 + t]).astype(BF16)
+        value = terms(slot_ref[0, 2 + t]).astype(BF16)
+        for r in range(chunks):
+            high1_ref[r][0, t] = value[r * depth : (r + 1) * depth]
     states_out_ref[0] = states_ref[...]
     pl.semaphore_wait(barrier, len(peers))
     high1 = [
-        send(high1_ref.at[0], high1_ref.at[d], place(0, high_peer(d))) for d in range(1, highs)
+        [
+            send(high1_ref[r].at[0], high1_ref[r].at[d], place(0, high_peer(d)))
+            for d in range(1, highs)
+        ]
+        for r in range(chunks)
     ]
     for t in range(2):
         term_ref[t] = terms(slot_ref[0, t]).astype(BF16)
@@ -135,7 +146,7 @@
     for p in range(block_len):
         lo, hi = p * states_count, (p + 1) * states_count
         mask = mask | ((row >= lo) & (row < hi) & (wide >= lo) & (wide < hi))
-    logits = fields_ref[...] + terms(jnp.where(mask, 0.0, diag_ref[0]))
+    logits_ref[...] = fields_ref[...] + terms(jnp.where(mask, 0.0, diag_ref[0]))
     same = jnp.where(mask, 1.0, 0.0).astype(BF16)
 
     def search(target, t):
@@ -150,83 +161,106 @@
             hit = hit | (partner_ref[pos, k] == holder)
         return jnp.where(hit & (holder >= 0), 1.0, 0.0).astype(F32)
 
-    holders = [search(pos, t) for t in range(slots)]
-
     def ring(value, size):
         return lax.rem(value + size, size)
 
-    for copy in high1:
-        copy.wait_recv()
-    low1 = []
-    for e in list(range(1, lows)) + [0]:
+    holders = [search(pos, t) for t in range(slots)]
+    alive = [listed(holder) for holder in holders]
+    order = list(range(1, lows)) + [0]
+    picks1, picks2 = {}, {}
+    for e in order:
+        target = low_peer(e)
         for t in range(far):
-            target = low_peer(e)
             pick = jnp.int32(0)
             for h in range(highs):
                 found = slot_blocks_ref[h * lows + low, 2 + t] == target
                 pick = jnp.where(found, ring(high - h, highs), pick)
-            value = high1_ref[pick, t]
-            if e == 0:
-                low1_ref[0, t] = value
-            else:
-                stage1_ref[e, t] = value
-        if e:
-            low1.append(send(stage1_ref.at[e], low1_ref.at[e], place(0, target)))
+            picks1[e, t] = pick
+            wanted = jnp.maximum(slot_blocks_ref[target, 2 + t], 0)
+            picks2[e, t] = ring(high - wanted // lows, highs)
+    weight = 1.0 / multiplicity_ref[...]
+
+    def pass_low(load, stage_ref, low_ref):
+        sent = []
+        for e in order:
+            for t in range(far):
+                value = load(e, t)
+                if e == 0:
+                    low_ref[0, t] = value
+                else:
+                    stage_ref[e, t] = value
+            if e:
+                sent.append(
+                    send(
+                        stage_ref.at[e],
+                        low_ref.at[e],
+                        place(0, low_peer(e)),
+                    )
+                )
+        return sent
+
+    low1 = []
+    for r in range(chunks):
+        for copy in high1[r]:
+            copy.wait_recv()
+        low1.append(
+            pass_low(lambda e, t: high1_ref[r][picks1[e, t], t], stage1_ref[r], low1_ref[r])
+        )
     for copy in near1:
         copy.wait_recv()
-    incoming = near_ref[0].astype(F32) * listed(holders[0])
-    incoming += near_ref[1].astype(F32) * listed(holders[1])
-    for copy in low1:
-        copy.wait_recv()
-    for t in range(far):
-        holder = holders[2 + t]
-        pick = ring(low - lax.rem(jnp.maximum(holder, 0), lows), lows)
-        incoming += low1_ref[pick, t].astype(F32) * listed(holder)
-    logits += incoming
-
-    peak = jnp.zeros_like(logits)
-    for p in range(block_len):
-        inside = start == p * states_count
-        top = jnp.max(jnp.where(inside, logits, -jnp.inf), axis=1, keepdims=True)
-        peak = jnp.where(inside, top, peak)
-    powers = jnp.exp(logits - peak)
-    first, second = halves(powers)
-    probabilities = powers / (times(first, same) + times(second, same))
-    weight = 1.0 / multiplicity_ref[...]
-    residual = (weight * (probabilities - onehot.astype(F32))).astype(BF16)
-    high2_ref[0] = residual
-    out_ref[0, slots] = residual
-
-    high2 = [
-        send(high2_ref.at[0], high2_ref.at[d], place(0, high_peer(d))) for d in range(1, highs)
-    ]
     slot_of = {0: slots, 1: 0, -1: 1}
-    last = [
-        send(high2_ref.at[0], out_ref.at[f, slot_of[g]], place(f, beside(g))) for f, g in near
-    ]
-    for copy in high2:
-        copy.wait_recv()
+    high2, last = [], []
+    column_start = start
+    for r, part in enumerate(parts):
+        logits = logits_ref[part] + near_ref[0, part].astype(F32) * alive[0]
+        logits += near_ref[1, part].astype(F32) * alive[1]
+        for copy in low1[r]:
+            copy.wait_recv()
+        for t in range(far):
+            holder = jnp.maximum(holders[2 + t], 0)
+            pick = ring(low - lax.rem(holder, lows), lows)
+            logits += low1_ref[r][pick, t].astype(F32) * alive[2 + t]
+        peak = jnp.zeros_like(logits)
+        for p in range(block_len):
+            inside = column_start == p * states_count
+            top = jnp.max(jnp.where(inside, logits, -jnp.inf), axis=1, keepdims=True)
+            peak = jnp.where(inside, top, peak)
+        powers = jnp.exp(logits - peak)
+        first, second = halves(powers)
+        probabilities = powers / (times(first, same) + times(second, same))
+        mine = slice(r * depth, (r + 1) * depth)
+        residual = (weight[mine] * (probabilities - onehot[mine].astype(F32))).astype(BF16)
+        high2_ref[r][0] = residual
+        out_ref[0, slots, part] = residual
+        high2.append(
+            [
+                send(high2_ref[r].at[0], high2_ref[r].at[d], place(0, high_peer(d)))
+                for d in range(1, highs)
+            ]
+        )
+        last += [
+            send(high2_ref[r].at[0], out_ref.at[f, slot_of[g], part], place(f, beside(g)))
+            for f, g in near
+        ]
     low2 = []
-    for e in list(range(1, lows)) + [0]:
+    for r in range(chunks):
+        for copy in high2[r]:
+            copy.wait_recv()
+        low2.append(
+            pass_low(lambda e, t: high2_ref[r][picks2[e, t]], stage2_ref[r], low2_ref[r])
+        )
+    ends = pl.ds(2, far)
+    for r, part in enumerate(parts):
+        for copy in low2[r]:
+            copy.wait_recv()
         for t in range(far):
-            target = low_peer(e)
-            wanted = jnp.maximum(slot_blocks_ref[target, 2 + t], 0)
-            value = high2_ref[ring(high - wanted // lows, highs)]
-            if e == 0:
-                low2_ref[0, t] = value
-            else:
-                stage2_ref[e, t] = value
-        if e:
-            low2.append(send(stage2_ref.at[e], low2_ref.at[e], place(0, target)))
-    for copy in low2:
-        copy.wait_recv()
-    for t in range(far):
-        wanted = jnp.maximum(slot_blocks_ref[pos, 2 + t], 0)
-        out_ref[0, 2 + t] = low2_ref[ring(low - lax.rem(wanted, lows), lows), t]
-    last += [
-        send(out_ref.at[0, pl.ds(2, far)], out_ref.at[f, pl.ds(2, far)], place(f, pos))
-        for f in range(1, seqs)
-    ]
+            wanted = jnp.maximum(slot_blocks_ref[pos, 2 + t], 0)
+            pick = ring(low - lax.rem(wanted, lows), lows)
+            out_ref[0, 2 + t, part] = low2_ref[r][pick, t]
+        last += [
+            send(out_ref.at[0, ends, part], out_ref.at[f, ends, part], place(f, pos))
+            for f in range(1, seqs)
+        ]
     for copy in states_moves + last:
         copy.wait_recv()
     for copy in copies:
@@ -240,11 +274,13 @@
     seqs, blocks = lax.axis_size("seq"), lax.axis_size("pos")
     lows = 4 if blocks % 4 == 0 else 1
     highs = blocks // lows
-    moves = 2 * (highs - 1) + 2 * (lows - 1) + 2 + (seqs - 1) * 2 + 3 * seqs
+    moves = 4 * (highs - 1) + 4 * (lows - 1) + 9 * seqs
     vmem = pl.BlockSpec(memory_space=pltpu.VMEM)
     smem = pl.BlockSpec(memory_space=pltpu.SMEM)
     far = slots - 2
     tile = (seq_rows, width)
+    chunks = 2 if seq_rows % 32 == 0 else 1
+    piece = (seq_rows // chunks, width)
     return pl.pallas_call(
         functools.partial(exchange_kernel, block_len, width // block_len, seqs, highs, lows),
         in_specs=[smem, smem, vmem, vmem, vmem, vmem, vmem],
@@ -256,12 +292,13 @@
         scratch_shapes=[
             pltpu.VMEM((2,) + tile, BF16),
             pltpu.VMEM((2,) + tile, BF16),
-            pltpu.VMEM((highs, far) + tile, BF16),
-            pltpu.VMEM((lows, far) + tile, BF16),
-            pltpu.VMEM((lows, far) + tile, BF16),
-            pltpu.VMEM((highs,) + tile, BF16),
-            pltpu.VMEM((lows, far) + tile, BF16),
-            pltpu.VMEM((lows, far) + tile, BF16),
+            [pltpu.VMEM((highs, far) + piece, BF16)] * chunks,
+            [pltpu.VMEM((lows, far) + piece, BF16)] * chunks,
+            [pltpu.VMEM((lows, far) + piece, BF16)] * chunks,
+            [pltpu.VMEM((highs,) + piece, BF16)] * chunks,
+            [pltpu.VMEM((lows, far) + piece, BF16)] * chunks,
+            [pltpu.VMEM((lows, far) + piece, BF16)] * chunks,
+            pltpu.VMEM(tile, F32),
             pltpu.SemaphoreType.DMA((moves,)),
             pltpu.SemaphoreType.DMA((moves,)),
         ],

time: 72.7 us -> 64.7 us (0.89)
  the two profiles are of different devices: /device:TPU:27 before, /device:TPU:11 now
where the time goes in v3:
time: 64.7 us; the launch traced here: 64.4 us
  Pallas kernels  56.6 us (87%)
  local copies, waits for them, and re-layouts  5.71 us (9%)
  other arithmetic  1.38 us (2%)
  between operations  0.65 us (1%)
    pallas_call x1, Pallas kernels, exchange(): pl.pallas_call(functools.partial(exchange_kernel, block_len, width // blo...  48.3 us
    pallas_call x1, Pallas kernels, apply_step(): pl.pallas_call(functools.partial(step_kernel, block_len, states_count, sl...  8.36 us
    unnamed x6, local copies, waits for them, and re-layouts  4.13 us

profile of v3, /device:TPU:11, one launch (start us, length us, event | category | flops | bytes accessed | tf_op | source)
XLA Modules:
  0.0 64.4 jit_solution(2822571278041827925)
XLA Ops:
  0.6 0.7 %convert_bitcast_fusion.1 = f32[128,1]{0,1:T(1,128)S(1)} fusion(s32[128]{0:T(128)} %param.8), kind=kLoop, calls=%fused_computation.1 | loop fusion | flops 128 | bytes 1024 | tf_op jit(solution)/shard_map/broadcast_in_dim | solution.py:416
  1.3 0.8 %reshape.12.fields_ref = f32[1,336]{1,0:T(1,128)S(1)} reshape(f32[16,21]{1,0:T(8,128)} %param.9) | data formatting | bytes 2688 | tf_op jit(solution)/shard_map/reshape | solution.py:411
  2.1 0.7 %convert_bitcast_fusion.states_ref = bf16[16,128]{1,0:T(8,128)(2,1)S(1)} fusion(s32[128,16]{0,1:T(8,128)} %param.7), kind=kLoop, calls=%fused_computation | loop fusion | flops 2048 | bytes 12288 | tf_op jit(solution)/shard_map/convert_element_type | solution.py:415
  2.8 0.8 %copy.13.slot_blocks_ref = s32[16,4]{1,0:T(8,128)S(1)} copy(s32[16,4]{0,1:T(4,128)} %param.12) | data formatting | bytes 512 | tf_op args[5]
  3.5 0.8 %copy.14.partner_ref = s32[16,4]{1,0:T(8,128)S(1)} copy(s32[16,4]{0,1:T(4,128)} %param.13) | data formatting | bytes 512 | tf_op args[6]
  4.3 0.1 copy.12.multiplicity_ref
  4.4 0.0 copy-start
  4.4 1.6 %copy-done = f32[1,4,336,336]{3,2,1,0:T(8,128)S(1)} copy-done((f32[1,4,336,336]{3,2,1,0:T(8,128)S(1)}, f32[1,4,336,336]{3,2,1,0:T(8,128)}, u32[]{:S(2)}) %copy-start) | copy-done | bytes 1806360
  6.0 0.0 copy-start.1
  6.0 1.0 %copy-done.1 = f32[1,336,336]{2,1,0:T(8,128)S(1)} copy-done((f32[1,336,336]{2,1,0:T(8,128)S(1)}, f32[1,336,336]{2,1,0:T(8,128)}, u32[]{:S(2)}) %copy-start.1) | copy-done | bytes 451608
  7.0 48.3 %shard_map.94 = (bf16[2,5,128,336]{3,2,1,0:T(8,128)(2,1)S(1)}, bf16[2,16,128]{2,1,0:T(8,128)(2,1)S(1)}) custom-call(s32[16,4]{1,0:T(8,128)S(1)} %copy.13.slot_blocks_ref, s32[16,4]{1,0:T(8,128)S(1)} %copy.14.partner_ref, bf16[16,128]{1,0:T(8,128)(2,1)S(1)} %convert_bitcast_fusion.states_ref, f32[128,1]{1,0:T(8,128)S(1)} %copy.12.multiplicity_ref, ...), custom_call_target="tpu_custom_call" | custom-call | tf_op jit(solution)/shard_map/pallas_call | solution.py:284
  55.3 8.4 %shard_map.95 = (f32[1,336]{1,0:T(1,128)S(1)}, f32[1,336,336]{2,1,0:T(8,128)}, f32[1,4,336,336]{3,2,1,0:T(8,128)}) custom-call(s32[16,4]{1,0:T(8,128)S(1)} %copy.13.slot_blocks_ref, s32[16,4]{1,0:T(8,128)S(1)} %copy.14.partner_ref, bf16[2,5,128,336]{3,2,1,0:T(8,128)(2,1)S(1)} %get-tuple-element.8.resid_ref, ...), custom_call_target="tpu_custom_call" | custom-call | tf_op jit(solution)/shard_map/pallas_call | solution.py:395
  63.7 0.7 %reshape.13 = f32[16,21]{1,0:T(8,128)} reshape(f32[336]{0:T(512)S(1)} %reduce) | data formatting | bytes 2688 | tf_op jit(solution)/shard_map/reshape | solution.py:405
  (1 shorter events, 0.0 us)
Async XLA Ops:
  4.4 1.6 %copy-start = (f32[1,4,336,336]{3,2,1,0:T(8,128)S(1)}, f32[1,4,336,336]{3,2,1,0:T(8,128)}, u32[]{:S(2)}) copy-start(f32[1,4,336,336]{3,2,1,0:T(8,128)} %slot_ref.3) | copy-start | bytes 5419012
  6.0 1.0 %copy-start.1 = (f32[1,336,336]{2,1,0:T(8,128)S(1)}, f32[1,336,336]{2,1,0:T(8,128)}, u32[]{:S(2)}) copy-start(f32[1,336,336]{2,1,0:T(8,128)} %diag_ref.3) | copy-start | bytes 1354756

commit v4 on v3

--- a/solution.py
+++ b/solution.py
@@ -39,6 +39,17 @@
     for p in range(1, block_len):
         start = jnp.where(column >= p * states_count, p * states_count, start)
     return column, start
+
+
+def row_of(fields, groups, column, start):
+    block_len, states_count = fields.shape
+    state = lax.broadcasted_iota(jnp.int32, (states_count, column.shape[1]), 0)
+    spread = jnp.where(state == column - start, 1.0, 0.0).astype(BF16)
+    first = fields.astype(BF16)
+    rest = fields - first.astype(F32)
+    second, third = halves(rest)
+    wide = times(third, spread) + times(second, spread) + times(first, spread)
+    return jnp.sum(wide * groups.astype(F32), axis=0, keepdims=True)
 
 
 def onehot_of(states_t, groups, column, start):
@@ -146,7 +157,7 @@
     for p in range(block_len):
         lo, hi = p * states_count, (p + 1) * states_count
         mask = mask | ((row >= lo) & (row < hi) & (wide >= lo) & (wide < hi))
-    logits_ref[...] = fields_ref[...] + terms(jnp.where(mask, 0.0, diag_ref[0]))
+    logits_ref[...] = row_of(fields_ref[...], groups, column, start) + terms(jnp.where(mask, 0.0, diag_ref[0]))
     same = jnp.where(mask, 1.0, 0.0).astype(BF16)
 
     def search(target, t):
@@ -178,7 +189,10 @@
             picks1[e, t] = pick
             wanted = jnp.maximum(slot_blocks_ref[target, 2 + t], 0)
             picks2[e, t] = ring(high - wanted // lows, highs)
-    weight = 1.0 / multiplicity_ref[...]
+    across = lax.broadcasted_iota(jnp.int32, (rows, rows), 0)
+    along = lax.broadcasted_iota(jnp.int32, (rows, rows), 1)
+    counts = jnp.where(across == along, multiplicity_ref[...], 0).astype(F32)
+    weight = 1.0 / jnp.sum(counts, axis=1, keepdims=True)
 
     def pass_low(load, stage_ref, low_ref):
         sent = []
@@ -269,17 +283,17 @@
 
 def exchange(slot_blocks, partner_blocks, states_t, multiplicity, fields, diag, slot):
     block_len, seq_rows = states_t.shape
-    width = fields.shape[1]
+    width = fields.size
     slots = slot.shape[1]
     seqs, blocks = lax.axis_size("seq"), lax.axis_size("pos")
     lows = 4 if blocks % 4 == 0 else 1
     highs = blocks // lows
-    moves = 4 * (highs - 1) + 4 * (lows - 1) + 9 * seqs
     vmem = pl.BlockSpec(memory_space=pltpu.VMEM)
     smem = pl.BlockSpec(memory_space=pltpu.SMEM)
     far = slots - 2
     tile = (seq_rows, width)
-    chunks = 2 if seq_rows % 32 == 0 else 1
+    chunks = 4 if seq_rows % 64 == 0 else 1
+    moves = 2 * chunks * (highs + lows) + (4 * chunks + 1) * seqs
     piece = (seq_rows // chunks, width)
     return pl.pallas_call(
         functools.partial(exchange_kernel, block_len, width // block_len, seqs, highs, lows),
@@ -366,7 +380,7 @@
         factor = jnp.where(row == column, 0.0, factors(values))
         new_diag_ref[0] = values * expand(factor)
         ones = jnp.ones((8, resid.shape[0]), BF16)
-        new_fields_ref[...] = fields_ref[...] - STEP_SIZE * times(ones, resid)[:1]
+        new_fields_ref[...] = row_of(fields_ref[...], groups, *position_starts(block_len, states_count)) - STEP_SIZE * times(ones, resid)[:1]
 
 
 def apply_step(slot_blocks, partner_blocks, gathered, states_all, fields, diag_couplings, slot_couplings):
@@ -381,7 +395,7 @@
         in_specs=[
             pl.BlockSpec((seqs, 1, seq_rows, width), lambda i, ids, alive: (0, i, 0, 0)),
             pl.BlockSpec(states_all.shape, lambda i, ids, alive: (0, 0, 0)),
-            pl.BlockSpec((1, width), lambda i, ids, alive: (0, 0)),
+            pl.BlockSpec(fields.shape, lambda i, ids, alive: (0, 0)),
             pl.BlockSpec((1, width, width), lambda i, ids, alive: (0, 0, 0)),
             pl.BlockSpec((1, 1, width, width), lambda i, ids, alive: (0, jnp.minimum(i, last), 0, 0)),
         ],
@@ -408,18 +422,17 @@
 def per_device(
     states, multiplicity, fields, diag_couplings, slot_couplings, slot_blocks, partner_blocks
 ):
-    fields_row = fields.reshape(1, -1)
     gathered, states_all = exchange(
         slot_blocks,
         partner_blocks,
         states.T.astype(BF16),
-        multiplicity.astype(F32)[:, None],
-        fields_row,
+        multiplicity[None, :],
+        fields,
         diag_couplings,
         slot_couplings,
     )
     return apply_step(
-        slot_blocks, partner_blocks, gathered, states_all, fields_row, diag_couplings, slot_couplings
+        slot_blocks, partner_blocks, gathered, states_all, fields, diag_couplings, slot_couplings
     )
 
 

time: 64.7 us -> 62.6 us (0.968)
  the two profiles are of different devices: /device:TPU:11 before, /device:TPU:0 now
where the time goes in v4:
time: 62.6 us; the launch traced here: 62.3 us
  Pallas kernels  54.7 us (87%)
  local copies, waits for them, and re-layouts  6.17 us (10%)
  other arithmetic  0.72 us (1%)
  between operations  0.64 us (1%)
    pallas_call x1, Pallas kernels, exchange(): pl.pallas_call(functools.partial(exchange_kernel, block_len, width // blo...  46.4 us
    pallas_call x1, Pallas kernels, apply_step(): pl.pallas_call(functools.partial(step_kernel, block_len, states_count, sl...  8.38 us
    unnamed x10, local copies, waits for them, and re-layouts  5.48 us

profile of v4, /device:TPU:0, one launch (start us, length us, event | category | flops | bytes accessed | tf_op | source)
XLA Modules:
  0.0 62.3 jit_solution(3096616148139899470)
XLA Ops:
  0.6 0.7 %convert_bitcast_fusion.states_ref = bf16[16,128]{1,0:T(8,128)(2,1)S(1)} fusion(s32[128,16]{0,1:T(8,128)} %param.7), kind=kLoop, calls=%fused_computation | loop fusion | flops 2048 | bytes 12288 | tf_op jit(solution)/shard_map/convert_element_type | solution.py:428
  1.3 0.8 %copy.12.slot_blocks_ref = s32[16,4]{1,0:T(8,128)S(1)} copy(s32[16,4]{0,1:T(4,128)} %param.12) | data formatting | bytes 512 | tf_op args[5]
  2.1 0.8 %copy.13.partner_ref = s32[16,4]{1,0:T(8,128)S(1)} copy(s32[16,4]{0,1:T(4,128)} %param.13) | data formatting | bytes 512 | tf_op args[6]
  2.8 0.0 copy-start
  2.8 1.6 %copy-done = f32[1,4,336,336]{3,2,1,0:T(8,128)S(1)} copy-done((f32[1,4,336,336]{3,2,1,0:T(8,128)S(1)}, f32[1,4,336,336]{3,2,1,0:T(8,128)}, u32[]{:S(2)}) %copy-start) | copy-done | bytes 1806360
  4.4 0.0 copy-start.1
  4.4 1.0 %copy-done.1 = f32[1,336,336]{2,1,0:T(8,128)S(1)} copy-done((f32[1,336,336]{2,1,0:T(8,128)S(1)}, f32[1,336,336]{2,1,0:T(8,128)}, u32[]{:S(2)}) %copy-start.1) | copy-done | bytes 451608
  5.5 0.0 copy-start.2
  5.5 0.7 %copy-done.2 = f32[16,21]{1,0:T(8,128)S(1)} copy-done((f32[16,21]{1,0:T(8,128)S(1)}, f32[16,21]{1,0:T(8,128)}, u32[]{:S(2)}) %copy-start.2) | copy-done | bytes 1368
  6.2 0.0 copy-start.3
  6.2 0.7 %copy-done.3 = s32[128]{0:T(128)S(1)} copy-done((s32[128]{0:T(128)S(1)}, s32[128]{0:T(128)}, u32[]{:S(2)}) %copy-start.3) | copy-done | bytes 536
  6.8 46.4 %shard_map.94 = (bf16[2,5,128,336]{3,2,1,0:T(8,128)(2,1)S(1)}, bf16[2,16,128]{2,1,0:T(8,128)(2,1)S(1)}) custom-call(s32[16,4]{1,0:T(8,128)S(1)} %copy.12.slot_blocks_ref, s32[16,4]{1,0:T(8,128)S(1)} %copy.13.partner_ref, bf16[16,128]{1,0:T(8,128)(2,1)S(1)} %convert_bitcast_fusion.states_ref, s32[1,128]{1,0:T(1,128)S(1)} %bitcast.3, f32[16,21]{1,0:T(8,128)S(1)} %copy-done.2, ...), custom_call_target="tpu_custom_call" | custom-call | tf_op jit(solution)/shard_map/pallas_call | solution.py:298
  53.2 8.4 %shard_map.95 = (f32[1,336]{1,0:T(1,128)S(1)}, f32[1,336,336]{2,1,0:T(8,128)}, f32[1,4,336,336]{3,2,1,0:T(8,128)}) custom-call(s32[16,4]{1,0:T(8,128)S(1)} %copy.12.slot_blocks_ref, s32[16,4]{1,0:T(8,128)S(1)} %copy.13.partner_ref, bf16[2,5,128,336]{3,2,1,0:T(8,128)(2,1)S(1)} %get-tuple-element.8.resid_ref, ...), custom_call_target="tpu_custom_call" | custom-call | tf_op jit(solution)/shard_map/pallas_call | solution.py:409
  61.6 0.7 %reshape.9 = f32[16,21]{1,0:T(8,128)} reshape(f32[336]{0:T(512)S(1)} %reduce) | data formatting | bytes 2688 | tf_op jit(solution)/shard_map/reshape | solution.py:419
  (1 shorter events, 0.0 us)
Async XLA Ops:
  2.8 1.6 %copy-start = (f32[1,4,336,336]{3,2,1,0:T(8,128)S(1)}, f32[1,4,336,336]{3,2,1,0:T(8,128)}, u32[]{:S(2)}) copy-start(f32[1,4,336,336]{3,2,1,0:T(8,128)} %slot_ref.3) | copy-start | bytes 5419012
  4.4 1.0 %copy-start.1 = (f32[1,336,336]{2,1,0:T(8,128)S(1)}, f32[1,336,336]{2,1,0:T(8,128)}, u32[]{:S(2)}) copy-start(f32[1,336,336]{2,1,0:T(8,128)} %diag_ref.3) | copy-start | bytes 1354756
  5.5 0.7 %copy-start.2 = (f32[16,21]{1,0:T(8,128)S(1)}, f32[16,21]{1,0:T(8,128)}, u32[]{:S(2)}) copy-start(f32[16,21]{1,0:T(8,128)} %fields_ref.3) | copy-start | bytes 4036
  6.2 0.7 %copy-start.3 = (s32[128]{0:T(128)S(1)}, s32[128]{0:T(128)}, u32[]{:S(2)}) copy-start(s32[128]{0:T(128)} %param.8) | copy-start | bytes 1540
